TPU v7x, 128 devices: a whole 4x4x4 slice. The times are simulated.
128 devices in a mesh: fsdp: 32 (over x, y, core), tp: 4 (over z).
Axes of the slice: x: 4, y: 4, z: 4, core: 2. Of those that a mesh axis runs over, the one named last changes fastest.
Arguments:
- gradient: float32 [8, 512, 14336], P(None, 'fsdp', 'tp'), may hold values from -200 to 200
- first_moment: float32 [64, 512, 2048], P('fsdp', None, 'tp'), may hold values from -4 to 4
- second_moment: float32 [64, 512, 2048], P('fsdp', None, 'tp'), may hold values from 0.01 to 1
- left_basis: float32 [64, 512, 2048], P('fsdp', None, 'tp'), may hold values from -0.25 to 0.25
- right_basis: float32 [64, 512, 2048], P('fsdp', None, 'tp'), may hold values from -0.25 to 0.25
- left_gram: float32 [64, 512, 2048], P('fsdp', None, 'tp'), may hold values from -6 to 6
- right_gram: float32 [64, 512, 2048], P('fsdp', None, 'tp'), may hold values from -6 to 6
- owner_slot: int32 [8, 28], P(None, 'tp'), may hold values from 0 to 63, as said below
Outputs:
- direction: float32 [8, 512, 14336], P(None, 'fsdp', 'tp')
- new_first: float32 [64, 512, 2048], P('fsdp', None, 'tp')
- new_second: float32 [64, 512, 2048], P('fsdp', None, 'tp')
- new_left_gram: float32 [64, 512, 2048], P('fsdp', None, 'tp')
- new_right_gram: float32 [64, 512, 2048], P('fsdp', None, 'tp')
Inputs may be any that keep to these rules, and one draw needn't show every extreme that they name: `owner_slot`: within the 7 block columns of one index of tp, all entries are distinct; slot s lies on index s // 2 of fsdp.
All inputs are finite; a program needn't handle non-finite values.
Results may differ from a plain program's by a relative error of at most 0.00007.
Values sent between devices are 32-bit elements; how exact they have to be, the bound alone decides.
A program may use at most 128 MiB of HBM per device.

v0:
```python
import functools
import math

import jax
import jax.numpy as jnp
from jax import lax
from jax.experimental import pallas as pl
from jax.experimental.pallas import tpu as pltpu
from jax.sharding import PartitionSpec as P

D = 4096
FF = 14336

first_beta = 0.9
second_beta = 0.95
gram_beta = 0.95
first_fix = 1.0 / (1.0 - 0.9**10)
second_fix = 1.0 / (1.0 - 0.95**10)
eps_value = 1e-08

MESH = pl.DeviceIdType.MESH
f32 = jnp.float32
bf16 = jnp.bfloat16

CHIP_STEPS = (
    (2, 2),
    (3, 2), (2, 3), (1, 2), (2, 1),
    (0, 2), (2, 0),
    (3, 1), (1, 3), (3, 3), (1, 1),
    (0, 3), (0, 1), (3, 0), (1, 0),
)
STEPS = tuple((a, b, c) for c in (0, 1) for a, b in CHIP_STEPS) + ((0, 0, 1),)
ROW_STEPS = (2, 1, 3, 0)


def split(value):
    high = value.astype(bf16)
    return high, (value - high.astype(f32)).astype(bf16)


def put(pair, rows, value):
    high, low = split(value)
    pair[0, rows, :] = high
    pair[1, rows, :] = low


def product(left, rows, right):
    left_high, left_low = left[0, rows, :], left[1, rows, :]
    right_high, right_low = right[0], right[1]
    total = jnp.dot(left_low, right_high, preferred_element_type=f32)
    total += jnp.dot(left_high, right_low, preferred_element_type=f32)
    return total + jnp.dot(left_high, right_high, preferred_element_type=f32)


def kernel(
    owner_in, gradient, first_in, second_in, left_in, right_in, left_stat, right_stat,
    returned, first, second, left_gram, right_gram,
    grad, packed, arrived, leaving, owner, places, block_at,
    left_raw, right_raw,
    left_basis, left_turned, right_basis, right_turned,
    block, turned, partial, normal, rotated,
    column_parts, row_parts, mine, factor,
    fetch_sem, place_sem, load_sem, column_send, column_recv, norm_send, norm_recv, in_send, in_recv, out_send, out_recv,
):
    devices, cols, size = 32, owner_in.shape[1], 512
    me = lax.axis_index("fsdp")
    tp = lax.axis_index("tp")
    my_x, my_y, my_core = me // 8, (me // 2) % 4, me % 2

    def place(step):
        a, b, c = step
        return ((my_x + a) % 4) * 8 + ((my_y + b) % 4) * 2 + (my_core + c) % 2

    loads = [
        pltpu.make_async_copy(source, target, load_sem.at[i])
        for i, (source, target) in enumerate((
            (left_in, left_raw), (right_in, right_raw), (first_in, first),
            (second_in, second), (left_stat, left_gram), (right_stat, right_gram),
        ))
    ]
    rows_b = gradient.shape[0]
    blocks = rows_b * cols
    fetches = [
        pltpu.make_async_copy(
            gradient.at[:, :, pl.ds(c * size, size)], grad.at[pl.ds(c * rows_b, rows_b)], fetch_sem.at[0]
        )
        for c in range(cols)
    ]
    fetch_owner = pltpu.make_async_copy(owner_in, owner, place_sem.at[1])
    fetch_owner.start()
    for fetch in fetches:
        fetch.start()
    grad[blocks] = jnp.zeros(grad.shape[1:], f32)

    barrier = pltpu.get_barrier_semaphore()

    def greet(k, _):
        pl.semaphore_signal(barrier, inc=1, device_id={"fsdp": (me + k) % devices}, device_id_type=MESH)
        return 0

    def greet_column(k, _):
        pl.semaphore_signal(barrier, inc=1, device_id={"tp": (tp + k) % 4}, device_id_type=MESH)
        return 0

    lax.fori_loop(1, devices, greet, 0)
    lax.fori_loop(1, 4, greet_column, 0)
    fetch_owner.wait()
    slots = lax.broadcasted_iota(jnp.int32, (rows_b, 128), 1)
    row = lax.broadcasted_iota(jnp.int32, (rows_b, 128), 0)
    found = jnp.full((rows_b, 128), -1, jnp.int32)
    for c in range(cols):
        found = jnp.maximum(found, jnp.where(owner[:, c:c + 1] == slots, row + c * rows_b, -1))
    found = jnp.max(found, axis=0, keepdims=True)
    found = jnp.where(found < 0, blocks, found)
    places[...] = jnp.broadcast_to(found, places.shape)
    to_scalars = pltpu.make_async_copy(places, block_at, place_sem.at[0])
    to_scalars.start()

    total = jnp.zeros((16, size), f32)
    whole = grad.at[pl.ds(0, blocks)]
    pltpu.make_async_copy(whole, whole, fetch_sem.at[0]).wait()

    def square(i, total):
        value = grad[i]
        return total + value * value

    total = lax.fori_loop(0, blocks, square, total, unroll=8)
    for load in loads:
        load.start()
    total = total[:8] + total[8:]
    total = total[:, 0:128] + total[:, 128:256] + total[:, 256:384] + total[:, 384:512]
    mine[0] = total
    column_parts[tp] = total
    to_scalars.wait()

    def pack(s, to):
        packed[s, to] = grad[block_at[0, 2 * to + s]]

    pl.semaphore_wait(barrier, devices - 1 + 3)

    def wait_all(view, send, recv):
        pltpu.make_async_remote_copy(
            src_ref=view, dst_ref=view, send_sem=send, recv_sem=recv,
            device_id={"fsdp": place((0, 0, 1))}, device_id_type=MESH,
        ).wait()

    def column_copy(k):
        return pltpu.make_async_remote_copy(
            src_ref=mine.at[0], dst_ref=column_parts.at[tp],
            send_sem=column_send.at[0], recv_sem=column_recv.at[0],
            device_id={"tp": (tp + k + 1) % 4}, device_id_type=MESH,
        )

    def in_copy(s, k):
        to = place(STEPS[k])
        return pltpu.make_async_remote_copy(
            src_ref=packed.at[s, to], dst_ref=arrived.at[s, me],
            send_sem=in_send.at[s], recv_sem=in_recv.at[s],
            device_id={"fsdp": to}, device_id_type=MESH,
        )

    def norm_copy(k):
        return pltpu.make_async_remote_copy(
            src_ref=mine.at[1], dst_ref=row_parts.at[me],
            send_sem=norm_send.at[0], recv_sem=norm_recv.at[0],
            device_id={"fsdp": place(STEPS[k])}, device_id_type=MESH,
        )

    def out_copy(s, a, b, c):
        to = ((my_x + a) % 4) * 8 + ((my_y + b) % 4) * 2 + (my_core + c) % 2
        return pltpu.make_async_remote_copy(
            src_ref=leaving.at[s, to], dst_ref=returned.at[2 * me + s],
            send_sem=out_send.at[s], recv_sem=out_recv.at[s],
            device_id={"fsdp": to}, device_id_type=MESH,
        )

    for k in range(3):
        column_copy(k).start()
    for k in range(len(STEPS)):
        pack(0, place(STEPS[k]))
        in_copy(0, k).start()
    wait_all(column_parts.at[pl.ds(0, 3)], column_send.at[0], column_recv.at[0])
    own = column_parts[0] + column_parts[1] + column_parts[2] + column_parts[3]
    mine[1] = own
    row_parts[me] = own
    for k in range(len(STEPS)):
        norm_copy(k).start()
    for k in range(len(STEPS)):
        pack(1, place(STEPS[k]))
        in_copy(1, k).start()
    for s in (0, 1):
        arrived[s, me] = grad[block_at[0, 2 * me + s]]

    loads[0].wait()
    loads[1].wait()

    def prepare(s, _):
        rows = pl.ds(0, size)
        left = left_raw[s]
        put(left_basis.at[s], rows, left)
        put(left_turned.at[s], rows, left.T)
        right = right_raw[s]
        put(right_basis.at[s], rows, right)
        put(right_turned.at[s], rows, right.T)
        return 0

    lax.fori_loop(0, 2, prepare, 0)
    for load in loads[2:]:
        load.wait()

    def piece(s, t):
        return arrived[s, pl.ds(t * 16, 16)].reshape(256, size)

    def rotate(s):
        wait_all(arrived.at[s, pl.ds(0, devices - 1)], in_send.at[s], in_recv.at[s])
        for t in range(2):
            put(block, pl.ds(t * 256, 256), piece(s, t))

        def to_partial(t, _):
            rows = pl.ds(pl.multiple_of(t * 256, 256), 256)
            put(partial, rows, product(left_turned.at[s], rows, block))
            return 0

        lax.fori_loop(0, 2, to_partial, 0)

        def to_rotated(t, _):
            rows = pl.ds(pl.multiple_of(t * 256, 256), 256)
            rotated[rows, :] = product(partial, rows, right_basis.at[s])
            return 0

        lax.fori_loop(0, 2, to_rotated, 0)

    def finish_norm():
        wait_all(row_parts.at[pl.ds(0, devices - 1)], norm_send.at[0], norm_recv.at[0])
        parts = row_parts[0]
        for d in range(1, devices):
            parts = parts + row_parts[d]
        norm_sq = jnp.sum(jnp.sum(parts, axis=0, keepdims=True), axis=1, keepdims=True)
        scale = jnp.minimum(1.0, math.sqrt(D * FF) / jnp.sqrt(norm_sq))
        factor[...] = jnp.broadcast_to(scale, factor.shape)

    def rest(s):
        def update(t, _):
            rows = pl.ds(pl.multiple_of(t * 64, 64), 64)
            turn = rotated[rows, :] * factor[0:1, :]
            first_next = first_beta * first[s, rows, :] + (1.0 - first_beta) * turn
            second_next = second_beta * second[s, rows, :] + (1.0 - second_beta) * turn * turn
            first[s, rows, :] = first_next
            second[s, rows, :] = second_next
            put(normal, rows, first_fix * first_next / (jnp.sqrt(second_fix * second_next) + eps_value))
            return 0

        lax.fori_loop(0, size // 64, update, 0)

        def to_partial(t, _):
            rows = pl.ds(pl.multiple_of(t * 256, 256), 256)
            put(partial, rows, product(left_basis.at[s], rows, normal))
            return 0

        lax.fori_loop(0, 2, to_partial, 0)

        for a in ROW_STEPS:
            to_x = (my_x + a) % 4
            rows = pl.ds(pl.multiple_of(to_x * 128, 128), 128)
            leaving[s, pl.ds(to_x * 8, 8)] = product(partial, rows, right_turned.at[s]).reshape(8, 16, size)
            for c in (0, 1):
                for b in ROW_STEPS:
                    if (a, b, c) != (0, 0, 0):
                        out_copy(s, a, b, c).start()
        returned[2 * me + s] = leaving[s, me]

    rotate(0)
    finish_norm()
    rest(0)
    rotate(1)
    rest(1)

    gram_scale = factor[0:1, :] * factor[0:1, :] * ((1.0 - gram_beta) / size)
    def grams(s, _):
        def load(t, _):
            rows = pl.ds(pl.multiple_of(t * 256, 256), 256)
            put(block, rows, piece(s, t))
            return 0

        lax.fori_loop(0, 2, load, 0)
        put(turned, pl.ds(0, size), arrived[s].reshape(size, size).T)

        def step(t, _):
            rows = pl.ds(pl.multiple_of(t * 256, 256), 256)
            left_gram[s, rows, :] = gram_beta * left_gram[s, rows, :] + gram_scale * product(block, rows, turned)
            right_gram[s, rows, :] = gram_beta * right_gram[s, rows, :] + gram_scale * product(turned, rows, block)
            return 0

        lax.fori_loop(0, 2, step, 0)
        return 0

    lax.fori_loop(0, 2, grams, 0)

    for s in (0, 1):
        wait_all(returned.at[pl.ds(0, devices - 1)], out_send.at[s], out_recv.at[s])


def store(
    owner_in, returned, first, second, left_gram, right_gram,
    direction, first_out, second_out, left_out, right_out,
    owner, owner_sem, sem, block_sem,
):
    rows_b, cols = owner_in.shape
    size = returned.shape[2]
    copies = [
        pltpu.make_async_copy(source, target, sem.at[i])
        for i, (source, target) in enumerate(
            ((first, first_out), (second, second_out), (left_gram, left_out), (right_gram, right_out))
        )
    ]

    def pick(i, c):
        return pltpu.make_async_copy(
            returned.at[owner[i, c]], direction.at[i, :, pl.ds(c * size, size)], block_sem.at[0]
        )

    fetch_owner = pltpu.make_async_copy(owner_in, owner, owner_sem.at[0])
    fetch_owner.start()
    for copy in copies:
        copy.start()
    fetch_owner.wait()
    for i in range(rows_b):
        for c in range(cols):
            pick(i, c).start()
    pltpu.make_async_copy(direction, direction, block_sem.at[0]).wait()
    for copy in copies:
        copy.wait()


def local(gradient, first_moment, second_moment, left_basis, right_basis, left_gram, right_gram, owner_slot):
    rows_b, sub_rows, width = gradient.shape
    slots_dev, size, _ = first_moment.shape
    devices = lax.axis_size("fsdp")
    cols = width // size
    state = jax.ShapeDtypeStruct(first_moment.shape, f32)
    hbm = pl.BlockSpec(memory_space=pltpu.HBM)
    vmem = pl.BlockSpec(memory_space=pltpu.VMEM)
    pieces = pltpu.VMEM((slots_dev, devices, sub_rows, size), f32)
    whole = pltpu.VMEM(first_moment.shape, f32)
    pair = pltpu.VMEM((2, size, size), bf16)
    pairs = pltpu.VMEM((slots_dev, 2, size, size), bf16)
    dma = pltpu.SemaphoreType.DMA
    results = pl.pallas_call(
        kernel,
        out_shape=(pltpu.VMEM((devices * slots_dev, sub_rows, size), f32),) + (whole,) * 4,
        in_specs=[hbm] * 8,
        out_specs=(vmem,) * 5,
        scratch_shapes=[
            pltpu.VMEM((rows_b * cols + 1, sub_rows, size), f32), pieces, pieces, pieces,
            pltpu.VMEM((rows_b, cols), jnp.int32), pltpu.VMEM((8, 128), jnp.int32), pltpu.SMEM((8, 128), jnp.int32),
            whole, whole,
            pairs, pairs, pairs, pairs,
            pair, pair, pair, pair, pltpu.VMEM((size, size), f32),
            pltpu.VMEM((4, 8, 128), f32), pltpu.VMEM((devices, 8, 128), f32),
            pltpu.VMEM((2, 8, 128), f32), pltpu.VMEM((8, size), f32),
            dma((1,)), dma((2,)), dma((6,)), dma((1,)), dma((1,)), dma((1,)), dma((1,)),
            dma((2,)), dma((2,)), dma((2,)), dma((2,)),
        ],
        compiler_params=pltpu.CompilerParams(
            collective_id=0, has_side_effects=True, vmem_limit_bytes=52 * 1024 * 1024
        ),
    )(owner_slot, gradient, first_moment, second_moment, left_basis, right_basis, left_gram, right_gram)
    return pl.pallas_call(
        store,
        out_shape=(jax.ShapeDtypeStruct(gradient.shape, f32), state, state, state, state),
        in_specs=[hbm] + [vmem] * 5,
        out_specs=(hbm,) * 5,
        scratch_shapes=[pltpu.SMEM((rows_b, cols), jnp.int32), dma((1,)), dma((4,)), dma((1,))],
        compiler_params=pltpu.CompilerParams(vmem_limit_bytes=16 * 1024 * 1024),
    )(owner_slot, *results)


def solution(mesh):
    in_specs = (
        P(None, "fsdp", "tp"),
        P("fsdp", None, "tp"),
        P("fsdp", None, "tp"),
        P("fsdp", None, "tp"),
        P("fsdp", None, "tp"),
        P("fsdp", None, "tp"),
        P("fsdp", None, "tp"),
        P(None, "tp"),
    )
    out_specs = (
        P(None, "fsdp", "tp"),
        P("fsdp", None, "tp"),
        P("fsdp", None, "tp"),
        P("fsdp", None, "tp"),
        P("fsdp", None, "tp"),
    )
    return jax.shard_map(local, mesh=mesh, in_specs=in_specs, out_specs=out_specs, check_vma=False)
```

profile of v0, /device:TPU:1, one launch (start us, length us, event | category | flops | bytes accessed | tf_op | source)
XLA Modules:
  0.0 61.4 jit_solution(8298526148014859309)
XLA Ops:
  0.6 0.0 copy-start
  0.6 56.9 %shard_map.119 = (f32[64,16,512]{2,1,0:T(8,128)S(1)}, f32[2,512,512]{2,1,0:T(8,128)S(1)}, f32[2,512,512]{2,1,0:T(8,128)S(1)}, f32[2,512,512]{2,1,0:T(8,128)S(1)}, f32[2,512,512]{2,1,0:T(8,128)S(1)}) custom-call(s32[8,7]{1,0:T(8,128)} %owner_in.3, f32[8,16,3584]{2,1,0:T(8,128)} %gradient.1, f32[2,512,512]{2,1,0:T(8,128)} %first_in.1, ...), custom_call_target="tpu_custom_call" | custom-call | tf_op jit(solution)/shard_map/pallas_call | solution.py:348
  57.5 0.0 copy-done
  57.5 3.8 %shard_map.120 = (f32[8,16,3584]{2,1,0:T(8,128)}, f32[2,512,512]{2,1,0:T(8,128)}, f32[2,512,512]{2,1,0:T(8,128)}, f32[2,512,512]{2,1,0:T(8,128)}, f32[2,512,512]{2,1,0:T(8,128)}) custom-call(s32[8,7]{1,0:T(8,128)S(1)} %copy-done, f32[64,16,512]{2,1,0:T(8,128)S(1)} %get-tuple-element.10.returned, f32[2,512,512]{2,1,0:T(8,128)S(1)} %get-tuple-element.11.first, ...), custom_call_target="tpu_custom_call" | custom-call | tf_op jit(solution)/shard_map/pallas_call | solution.py:368
Async XLA Ops:
  0.6 56.9 %copy-start = (s32[8,7]{1,0:T(8,128)S(1)}, s32[8,7]{1,0:T(8,128)}, u32[]{:S(2)}) copy-start(s32[8,7]{1,0:T(8,128)} %owner_in.3) | copy-start | bytes 676
where the time goes:
time: 61.5 us; the launch traced here: 61.4 us
  Pallas kernels  60.7 us (99%)
  between operations  0.66 us (1%)
    pallas_call x1, Pallas kernels, local(): pl.pallas_call(kernel, out_shape=(pltpu.VMEM((devices * slots_dev, sub_ro...  56.9 us
    pallas_call x1, Pallas kernels, local(): pl.pallas_call(store, out_shape=(jax.ShapeDtypeStruct(gradient.shape, f32...  3.84 us

commit v1 on v0

--- a/solution.py
+++ b/solution.py
@@ -94,15 +94,12 @@
 
     barrier = pltpu.get_barrier_semaphore()
 
-    def greet(k, _):
-        pl.semaphore_signal(barrier, inc=1, device_id={"fsdp": (me + k) % devices}, device_id_type=MESH)
-        return 0
-
     def greet_column(k, _):
         pl.semaphore_signal(barrier, inc=1, device_id={"tp": (tp + k) % 4}, device_id_type=MESH)
         return 0
 
-    lax.fori_loop(1, devices, greet, 0)
+    for step in STEPS:
+        pl.semaphore_signal(barrier, inc=1, device_id={"fsdp": place(step)}, device_id_type=MESH)
     lax.fori_loop(1, 4, greet_column, 0)
     fetch_owner.wait()
     slots = lax.broadcasted_iota(jnp.int32, (rows_b, 128), 1)
@@ -127,7 +124,7 @@
     total = lax.fori_loop(0, blocks, square, total, unroll=8)
     for load in loads:
         load.start()
-    total = total[:8] + total[8:]
+    total = jnp.sum(total, axis=0, keepdims=True)
     total = total[:, 0:128] + total[:, 128:256] + total[:, 256:384] + total[:, 384:512]
     mine[0] = total
     column_parts[tp] = total
@@ -232,10 +229,7 @@
 
     def finish_norm():
         wait_all(row_parts.at[pl.ds(0, devices - 1)], norm_send.at[0], norm_recv.at[0])
-        parts = row_parts[0]
-        for d in range(1, devices):
-            parts = parts + row_parts[d]
-        norm_sq = jnp.sum(jnp.sum(parts, axis=0, keepdims=True), axis=1, keepdims=True)
+        norm_sq = jnp.sum(jnp.sum(row_parts[...], axis=0), axis=1, keepdims=True)
         scale = jnp.minimum(1.0, math.sqrt(D * FF) / jnp.sqrt(norm_sq))
         factor[...] = jnp.broadcast_to(scale, factor.shape)
 
@@ -356,8 +350,8 @@
             whole, whole,
             pairs, pairs, pairs, pairs,
             pair, pair, pair, pair, pltpu.VMEM((size, size), f32),
-            pltpu.VMEM((4, 8, 128), f32), pltpu.VMEM((devices, 8, 128), f32),
-            pltpu.VMEM((2, 8, 128), f32), pltpu.VMEM((8, size), f32),
+            pltpu.VMEM((4, 1, 128), f32), pltpu.VMEM((devices, 1, 128), f32),
+            pltpu.VMEM((2, 1, 128), f32), pltpu.VMEM((8, size), f32),
             dma((1,)), dma((2,)), dma((6,)), dma((1,)), dma((1,)), dma((1,)), dma((1,)),
             dma((2,)), dma((2,)), dma((2,)), dma((2,)),
         ],

time: 61.5 us -> 60.1 us (0.977)
  Pallas kernels: 60.7 us -> 59.3 us
    pallas_call x1, Pallas kernels: 56.9 us -> 55.4 us  [local(): pl.pallas_call(kernel, out_shape=(pltpu.VMEM((devices * slots_dev, sub_ro...]
where the time goes in v1:
time: 60.1 us; the launch traced here: 59.9 us
  Pallas kernels  59.3 us (99%)
  between operations  0.66 us (1%)
    pallas_call x1, Pallas kernels, local(): pl.pallas_call(kernel, out_shape=(pltpu.VMEM((devices * slots_dev, sub_ro...  55.4 us
    pallas_call x1, Pallas kernels, local(): pl.pallas_call(store, out_shape=(jax.ShapeDtypeStruct(gradient.shape, f32...  3.84 us

profile of v1, /device:TPU:1, one launch (start us, length us, event | category | flops | bytes accessed | tf_op | source)
XLA Modules:
  0.0 59.9 jit_solution(1939128681522915344)
XLA Ops:
  0.6 0.0 copy-start
  0.6 55.4 %shard_map.119 = (f32[64,16,512]{2,1,0:T(8,128)S(1)}, f32[2,512,512]{2,1,0:T(8,128)S(1)}, f32[2,512,512]{2,1,0:T(8,128)S(1)}, f32[2,512,512]{2,1,0:T(8,128)S(1)}, f32[2,512,512]{2,1,0:T(8,128)S(1)}) custom-call(s32[8,7]{1,0:T(8,128)} %owner_in.3, f32[8,16,3584]{2,1,0:T(8,128)} %gradient.1, f32[2,512,512]{2,1,0:T(8,128)} %first_in.1, ...), custom_call_target="tpu_custom_call" | custom-call | tf_op jit(solution)/shard_map/pallas_call | solution.py:342
  56.1 0.0 copy-done
  56.1 3.8 %shard_map.120 = (f32[8,16,3584]{2,1,0:T(8,128)}, f32[2,512,512]{2,1,0:T(8,128)}, f32[2,512,512]{2,1,0:T(8,128)}, f32[2,512,512]{2,1,0:T(8,128)}, f32[2,512,512]{2,1,0:T(8,128)}) custom-call(s32[8,7]{1,0:T(8,128)S(1)} %copy-done, f32[64,16,512]{2,1,0:T(8,128)S(1)} %get-tuple-element.10.returned, f32[2,512,512]{2,1,0:T(8,128)S(1)} %get-tuple-element.11.first, ...), custom_call_target="tpu_custom_call" | custom-call | tf_op jit(solution)/shard_map/pallas_call | solution.py:362
Async XLA Ops:
  0.6 55.5 %copy-start = (s32[8,7]{1,0:T(8,128)S(1)}, s32[8,7]{1,0:T(8,128)}, u32[]{:S(2)}) copy-start(s32[8,7]{1,0:T(8,128)} %owner_in.3) | copy-start | bytes 676

commit v2 on v1

--- a/solution.py
+++ b/solution.py
@@ -31,6 +31,7 @@
 )
 STEPS = tuple((a, b, c) for c in (0, 1) for a, b in CHIP_STEPS) + ((0, 0, 1),)
 ROW_STEPS = (2, 1, 3, 0)
+FIRST = 22
 
 
 def split(value):
@@ -59,12 +60,13 @@
     left_raw, right_raw,
     left_basis, left_turned, right_basis, right_turned,
     block, turned, partial, normal, rotated,
-    column_parts, row_parts, mine, factor,
+    column_parts, row_parts, mine, norm, factor,
     fetch_sem, place_sem, load_sem, column_send, column_recv, norm_send, norm_recv, in_send, in_recv, out_send, out_recv,
 ):
     devices, cols, size = 32, owner_in.shape[1], 512
     me = lax.axis_index("fsdp")
     tp = lax.axis_index("tp")
+    gathers = me == 0
     my_x, my_y, my_core = me // 8, (me // 2) % 4, me % 2
 
     def place(step):
@@ -100,7 +102,11 @@
 
     for step in STEPS:
         pl.semaphore_signal(barrier, inc=1, device_id={"fsdp": place(step)}, device_id_type=MESH)
-    lax.fori_loop(1, 4, greet_column, 0)
+
+    @pl.when(gathers)
+    def _():
+        lax.fori_loop(1, 4, greet_column, 0)
+
     fetch_owner.wait()
     slots = lax.broadcasted_iota(jnp.int32, (rows_b, 128), 1)
     row = lax.broadcasted_iota(jnp.int32, (rows_b, 128), 0)
@@ -126,14 +132,20 @@
         load.start()
     total = jnp.sum(total, axis=0, keepdims=True)
     total = total[:, 0:128] + total[:, 128:256] + total[:, 256:384] + total[:, 384:512]
-    mine[0] = total
-    column_parts[tp] = total
+    mine[...] = total
+    row_parts[me] = total
     to_scalars.wait()
 
     def pack(s, to):
         packed[s, to] = grad[block_at[0, 2 * to + s]]
 
-    pl.semaphore_wait(barrier, devices - 1 + 3)
+    @pl.when(gathers)
+    def _():
+        pl.semaphore_wait(barrier, devices - 1 + 3)
+
+    @pl.when(jnp.logical_not(gathers))
+    def _():
+        pl.semaphore_wait(barrier, devices - 1)
 
     def wait_all(view, send, recv):
         pltpu.make_async_remote_copy(
@@ -143,7 +155,7 @@
 
     def column_copy(k):
         return pltpu.make_async_remote_copy(
-            src_ref=mine.at[0], dst_ref=column_parts.at[tp],
+            src_ref=mine, dst_ref=column_parts.at[tp],
             send_sem=column_send.at[0], recv_sem=column_recv.at[0],
             device_id={"tp": (tp + k + 1) % 4}, device_id_type=MESH,
         )
@@ -156,11 +168,18 @@
             device_id={"fsdp": to}, device_id_type=MESH,
         )
 
-    def norm_copy(k):
+    def part_copy():
         return pltpu.make_async_remote_copy(
-            src_ref=mine.at[1], dst_ref=row_parts.at[me],
+            src_ref=mine, dst_ref=row_parts.at[me],
             send_sem=norm_send.at[0], recv_sem=norm_recv.at[0],
-            device_id={"fsdp": place(STEPS[k])}, device_id_type=MESH,
+            device_id={"fsdp": 0}, device_id_type=MESH,
+        )
+
+    def norm_copy(step):
+        return pltpu.make_async_remote_copy(
+            src_ref=norm, dst_ref=norm,
+            send_sem=norm_send.at[1], recv_sem=norm_recv.at[1],
+            device_id={"fsdp": place(step)}, device_id_type=MESH,
         )
 
     def out_copy(s, a, b, c):
@@ -171,17 +190,35 @@
             device_id={"fsdp": to}, device_id_type=MESH,
         )
 
-    for k in range(3):
-        column_copy(k).start()
-    for k in range(len(STEPS)):
+    @pl.when(jnp.logical_not(gathers))
+    def _():
+        part_copy().start()
+
+    for k in range(FIRST):
         pack(0, place(STEPS[k]))
         in_copy(0, k).start()
-    wait_all(column_parts.at[pl.ds(0, 3)], column_send.at[0], column_recv.at[0])
-    own = column_parts[0] + column_parts[1] + column_parts[2] + column_parts[3]
-    mine[1] = own
-    row_parts[me] = own
-    for k in range(len(STEPS)):
-        norm_copy(k).start()
+
+    @pl.when(gathers)
+    def _():
+        view = row_parts.at[pl.ds(0, devices - 1)]
+        pltpu.make_async_copy(view, view, norm_recv.at[0]).wait()
+        plane = jnp.sum(row_parts[...], axis=0)
+        mine[...] = plane
+        column_parts[tp] = plane
+        for k in range(3):
+            column_copy(k).start()
+
+    for k in range(FIRST, len(STEPS)):
+        pack(0, place(STEPS[k]))
+        in_copy(0, k).start()
+
+    @pl.when(gathers)
+    def _():
+        wait_all(column_parts.at[pl.ds(0, 3)], column_send.at[0], column_recv.at[0])
+        norm[...] = column_parts[0] + column_parts[1] + column_parts[2] + column_parts[3]
+        for step in STEPS:
+            norm_copy(step).start()
+
     for k in range(len(STEPS)):
         pack(1, place(STEPS[k]))
         in_copy(1, k).start()
@@ -228,8 +265,17 @@
         lax.fori_loop(0, 2, to_rotated, 0)
 
     def finish_norm():
-        wait_all(row_parts.at[pl.ds(0, devices - 1)], norm_send.at[0], norm_recv.at[0])
-        norm_sq = jnp.sum(jnp.sum(row_parts[...], axis=0), axis=1, keepdims=True)
+        @pl.when(gathers)
+        def _():
+            view = row_parts.at[pl.ds(0, devices - 1)]
+            pltpu.make_async_copy(view, view, norm_send.at[1]).wait()
+
+        @pl.when(jnp.logical_not(gathers))
+        def _():
+            part_copy().wait_send()
+            norm_copy(STEPS[0]).wait_recv()
+
+        norm_sq = jnp.sum(norm[...], axis=1, keepdims=True)
         scale = jnp.minimum(1.0, math.sqrt(D * FF) / jnp.sqrt(norm_sq))
         factor[...] = jnp.broadcast_to(scale, factor.shape)
 
@@ -351,8 +397,8 @@
             pairs, pairs, pairs, pairs,
             pair, pair, pair, pair, pltpu.VMEM((size, size), f32),
             pltpu.VMEM((4, 1, 128), f32), pltpu.VMEM((devices, 1, 128), f32),
-            pltpu.VMEM((2, 1, 128), f32), pltpu.VMEM((8, size), f32),
-            dma((1,)), dma((2,)), dma((6,)), dma((1,)), dma((1,)), dma((1,)), dma((1,)),
+            pltpu.VMEM((1, 128), f32), pltpu.VMEM((1, 128), f32), pltpu.VMEM((8, size), f32),
+            dma((1,)), dma((2,)), dma((6,)), dma((1,)), dma((1,)), dma((2,)), dma((2,)),
             dma((2,)), dma((2,)), dma((2,)), dma((2,)),
         ],
         compiler_params=pltpu.CompilerParams(

time: 60.1 us -> 58.8 us (0.978)
  Pallas kernels: 59.3 us -> 58 us
    pallas_call x1, Pallas kernels: 55.4 us -> 54.2 us  [local(): pl.pallas_call(kernel, out_shape=(pltpu.VMEM((devices * slots_dev, sub_ro...]
where the time goes in v2:
time: 58.8 us; the launch traced here: 58.7 us
  Pallas kernels  58 us (99%)
  between operations  0.66 us (1%)
    pallas_call x1, Pallas kernels, local(): pl.pallas_call(kernel, out_shape=(pltpu.VMEM((devices * slots_dev, sub_ro...  54.2 us
    pallas_call x1, Pallas kernels, local(): pl.pallas_call(store, out_shape=(jax.ShapeDtypeStruct(gradient.shape, f32...  3.84 us

profile of v2, /device:TPU:1, one launch (start us, length us, event | category | flops | bytes accessed | tf_op | source)
XLA Modules:
  0.0 58.7 jit_solution(6018093482415905885)
XLA Ops:
  0.6 0.0 copy-start
  0.6 54.2 %shard_map.119 = (f32[64,16,512]{2,1,0:T(8,128)S(1)}, f32[2,512,512]{2,1,0:T(8,128)S(1)}, f32[2,512,512]{2,1,0:T(8,128)S(1)}, f32[2,512,512]{2,1,0:T(8,128)S(1)}, f32[2,512,512]{2,1,0:T(8,128)S(1)}) custom-call(s32[8,7]{1,0:T(8,128)} %owner_in.3, f32[8,16,3584]{2,1,0:T(8,128)} %gradient.1, f32[2,512,512]{2,1,0:T(8,128)} %first_in.1, ...), custom_call_target="tpu_custom_call" | custom-call | tf_op jit(solution)/shard_map/pallas_call | solution.py:388
  54.9 0.0 copy-done
  54.9 3.8 %shard_map.120 = (f32[8,16,3584]{2,1,0:T(8,128)}, f32[2,512,512]{2,1,0:T(8,128)}, f32[2,512,512]{2,1,0:T(8,128)}, f32[2,512,512]{2,1,0:T(8,128)}, f32[2,512,512]{2,1,0:T(8,128)}) custom-call(s32[8,7]{1,0:T(8,128)S(1)} %copy-done, f32[64,16,512]{2,1,0:T(8,128)S(1)} %get-tuple-element.10.returned, f32[2,512,512]{2,1,0:T(8,128)S(1)} %get-tuple-element.11.first, ...), custom_call_target="tpu_custom_call" | custom-call | tf_op jit(solution)/shard_map/pallas_call | solution.py:408
Async XLA Ops:
  0.6 54.2 %copy-start = (s32[8,7]{1,0:T(8,128)S(1)}, s32[8,7]{1,0:T(8,128)}, u32[]{:S(2)}) copy-start(s32[8,7]{1,0:T(8,128)} %owner_in.3) | copy-start | bytes 676

commit v3 on v2

--- a/solution.py
+++ b/solution.py
@@ -73,6 +73,19 @@
         a, b, c = step
         return ((my_x + a) % 4) * 8 + ((my_y + b) % 4) * 2 + (my_core + c) % 2
 
+    barrier = pltpu.get_barrier_semaphore()
+
+    def greet_column(k, _):
+        pl.semaphore_signal(barrier, inc=1, device_id={"tp": (tp + k) % 4}, device_id_type=MESH)
+        return 0
+
+    for step in STEPS:
+        pl.semaphore_signal(barrier, inc=1, device_id={"fsdp": place(step)}, device_id_type=MESH)
+
+    @pl.when(gathers)
+    def _():
+        lax.fori_loop(1, 4, greet_column, 0)
+
     loads = [
         pltpu.make_async_copy(source, target, load_sem.at[i])
         for i, (source, target) in enumerate((
@@ -93,19 +106,6 @@
     for fetch in fetches:
         fetch.start()
     grad[blocks] = jnp.zeros(grad.shape[1:], f32)
-
-    barrier = pltpu.get_barrier_semaphore()
-
-    def greet_column(k, _):
-        pl.semaphore_signal(barrier, inc=1, device_id={"tp": (tp + k) % 4}, device_id_type=MESH)
-        return 0
-
-    for step in STEPS:
-        pl.semaphore_signal(barrier, inc=1, device_id={"fsdp": place(step)}, device_id_type=MESH)
-
-    @pl.when(gathers)
-    def _():
-        lax.fori_loop(1, 4, greet_column, 0)
 
     fetch_owner.wait()
     slots = lax.broadcasted_iota(jnp.int32, (rows_b, 128), 1)

time: 58.8 us -> 58.8 us (level)
  no operation moved by 1% of the time
where the time goes in v3:
time: 58.8 us; the launch traced here: 58.7 us
  Pallas kernels  58 us (99%)
  between operations  0.66 us (1%)
    pallas_call x1, Pallas kernels, local(): pl.pallas_call(kernel, out_shape=(pltpu.VMEM((devices * slots_dev, sub_ro...  54.2 us
    pallas_call x1, Pallas kernels, local(): pl.pallas_call(store, out_shape=(jax.ShapeDtypeStruct(gradient.shape, f32...  3.84 us

profile of v3, /device:TPU:1, one launch (start us, length us, event | category | flops | bytes accessed | tf_op | source)
XLA Modules:
  0.0 58.7 jit_solution(13833332667547897859)
XLA Ops:
  0.6 0.0 copy-start
  0.6 54.2 %shard_map.119 = (f32[64,16,512]{2,1,0:T(8,128)S(1)}, f32[2,512,512]{2,1,0:T(8,128)S(1)}, f32[2,512,512]{2,1,0:T(8,128)S(1)}, f32[2,512,512]{2,1,0:T(8,128)S(1)}, f32[2,512,512]{2,1,0:T(8,128)S(1)}) custom-call(s32[8,7]{1,0:T(8,128)} %owner_in.3, f32[8,16,3584]{2,1,0:T(8,128)} %gradient.1, f32[2,512,512]{2,1,0:T(8,128)} %first_in.1, ...), custom_call_target="tpu_custom_call" | custom-call | tf_op jit(solution)/shard_map/pallas_call | solution.py:388
  54.8 0.0 copy-done
  54.8 3.8 %shard_map.120 = (f32[8,16,3584]{2,1,0:T(8,128)}, f32[2,512,512]{2,1,0:T(8,128)}, f32[2,512,512]{2,1,0:T(8,128)}, f32[2,512,512]{2,1,0:T(8,128)}, f32[2,512,512]{2,1,0:T(8,128)}) custom-call(s32[8,7]{1,0:T(8,128)S(1)} %copy-done, f32[64,16,512]{2,1,0:T(8,128)S(1)} %get-tuple-element.10.returned, f32[2,512,512]{2,1,0:T(8,128)S(1)} %get-tuple-element.11.first, ...), custom_call_target="tpu_custom_call" | custom-call | tf_op jit(solution)/shard_map/pallas_call | solution.py:408
Async XLA Ops:
  0.6 54.2 %copy-start = (s32[8,7]{1,0:T(8,128)S(1)}, s32[8,7]{1,0:T(8,128)}, u32[]{:S(2)}) copy-start(s32[8,7]{1,0:T(8,128)} %owner_in.3) | copy-start | bytes 676
